TPU v7x, 32 devices: a whole 2x2x4 slice. The times are simulated.
32 devices in a mesh: batch: 16 (over z, x, core), tensor: 2 (over y).
Axes of the slice: x: 2, y: 2, z: 4, core: 2. Of those that a mesh axis runs over, the one named last changes fastest.
Arguments:
- residual: float32 [16, 1024, 2048], P('batch', 'tensor'), may hold values from -6 to 6
- segment_ids: int32 [16, 1024], P('batch'), may hold values from 0 to 3, never falling along the last dimension, each value on 1 to 512 neighbouring positions
- norm_gain: float32 [2048], replicated, may hold values from 0.5 to 1.5
- zgate_proj: bfloat16 [2048, 4096], P(None, 'tensor'), may hold values from -0.125 to 0.125
- xin_proj: bfloat16 [2048, 4096], P(None, 'tensor'), may hold values from -0.125 to 0.125
- bc_proj: bfloat16 [2048, 256], replicated, may hold values from -0.125 to 0.125
- dt_proj: bfloat16 [2048, 64], P(None, 'tensor'), may hold values from -0.125 to 0.125
- xconv_weight: float32 [4, 4096], P(None, 'tensor'), may hold values from -3 to 3
- xconv_bias: float32 [4096], P('tensor'), may hold values from -3 to 3
- bcconv_weight: float32 [4, 256], replicated, may hold values from -3 to 3
- bcconv_bias: float32 [256], replicated, may hold values from -3 to 3
- dt_bias: float32 [64], P('tensor'), may hold values from -4 to -1
- decay_log: float32 [64], P('tensor'), may hold values from -4 to 2
- skip_scale: float32 [64], P('tensor'), may hold values from 0.5 to 1.5
- gate_gain: float32 [4096], P('tensor'), may hold values from 0.5 to 1.5
- out_proj: bfloat16 [4096, 2048], P('tensor'), may hold values from -0.09375 to 0.09375
- cotangent: float32 [16, 1024, 2048], P('batch', 'tensor'), may hold values from -6 to 6
Outputs:
- block_output: float32 [16, 1024, 2048], P('batch', 'tensor')
- input_grad: float32 [16, 1024, 2048], P('batch', 'tensor')
- normgain_grad: float32 [2048], replicated
- zproj_grad: float32 [2048, 4096], P(None, 'tensor')
- xproj_grad: float32 [2048, 4096], P(None, 'tensor')
- bcproj_grad: float32 [2048, 256], replicated
- dtproj_grad: float32 [2048, 64], P(None, 'tensor')
- xconv_grad: float32 [4, 4096], P(None, 'tensor')
- xbias_grad: float32 [4096], P('tensor')
- bcconv_grad: float32 [4, 256], replicated
- bcbias_grad: float32 [256], replicated
- dtbias_grad: float32 [64], P('tensor')
- decay_grad: float32 [64], P('tensor')
- skip_grad: float32 [64], P('tensor')
- gategain_grad: float32 [4096], P('tensor')
- outproj_grad: float32 [4096, 2048], P('tensor')
Inputs may be any that keep to these rules, and one draw needn't show every extreme that they name: `segment_ids`: along each row the numbers never fall; each document holds 1 to 512 positions and one holds exactly 512.
All inputs are finite; a program needn't handle non-finite values.
Results may differ from a plain program's by a relative error of at most 0.0089.
Values may be sent and summed in bfloat16 or wider, within the bound.
No kernel may reach another device: no remote copies, remote signals or barrier semaphores. Data moves between devices by JAX's collectives and lax.ppermute only.
A program may use at most 320 MiB of HBM per device.

v0:
```python
import jax
import jax.numpy as jnp
from jax import lax
from jax.sharding import PartitionSpec as P

DI = 4096
GROUP = 256


EPSILON = 1e-05
HIGHEST = lax.Precision.HIGHEST


def causal_conv(values, weight, offset, segments):
    summed = offset + weight[0] * values
    for delay_step in range(1, weight.shape[0]):
        shifted = jnp.pad(values, ((0, 0), (delay_step, 0), (0, 0)))[:, :-delay_step]
        earlier = jnp.pad(segments, ((0, 0), (delay_step, 0)), constant_values=-1)[:, :-delay_step]
        summed = summed + weight[delay_step] * jnp.where(
            (earlier == segments)[..., None], shifted, 0.0
        )
    return summed


def mixer(
    x_raw,
    bc_raw,
    dt_raw,
    z_raw,
    xconv_weight,
    xconv_bias,
    bcconv_weight,
    bcconv_bias,
    dt_bias,
    decay_log,
    skip_scale,
    segments,
    block_len,
):
    xconv = jax.nn.silu(causal_conv(x_raw, xconv_weight, xconv_bias, segments))
    bcconv = jax.nn.silu(causal_conv(bc_raw, bcconv_weight, bcconv_bias, segments))
    row_count, length, channels = xconv.shape
    head_count = dt_raw.shape[-1]
    head_size = channels // head_count
    state_size = bcconv.shape[-1] // 2
    block_count = length // block_len
    time_step = jax.nn.softplus(dt_raw + dt_bias)
    logdecay = -jnp.exp(decay_log) * time_step
    heads_view = xconv.reshape(row_count, length, head_count, head_size)
    values = (heads_view * time_step[..., None]).reshape(
        row_count, block_count, block_len, head_count, head_size
    )
    keys = bcconv[..., :state_size].reshape(row_count, block_count, block_len, state_size)
    queries = bcconv[..., state_size:].reshape(row_count, block_count, block_len, state_size)
    cumlog = jnp.cumsum(logdecay.reshape(row_count, block_count, block_len, head_count), axis=2)
    blocksegs = segments.reshape(row_count, block_count, block_len)
    positions = jnp.arange(block_len)
    causal = positions[:, None] >= positions[None, :]
    same_doc = (blocksegs[:, :, :, None] == blocksegs[:, :, None, :]) & causal
    scores = jnp.einsum("rctn,rcsn->rcts", queries, keys, precision=HIGHEST)
    log_gap = cumlog[:, :, :, None, :] - cumlog[:, :, None, :, :]
    mixing = jnp.exp(jnp.where(same_doc[..., None], log_gap, -jnp.inf)) * scores[..., None]
    intra = jnp.einsum("rctsh,rcshp->rcthp", mixing, values, precision=HIGHEST)
    last_seg = blocksegs[:, :, -1]
    to_end = jnp.exp(
        jnp.where(
            (blocksegs == last_seg[:, :, None])[..., None], cumlog[:, :, -1:, :] - cumlog, -jnp.inf
        )
    )
    weighted = values * to_end[..., None]
    local_state = jnp.einsum("rcshp,rcsn->rchpn", weighted, keys, precision=HIGHEST)
    prev_seg = jnp.concatenate([jnp.full((row_count, 1), -1, jnp.int32), last_seg[:, :-1]], axis=1)
    decay_gate = jnp.where((last_seg == prev_seg)[..., None], jnp.exp(cumlog[:, :, -1, :]), 0.0)

    def advance(carried, inputs):
        gate_now, state_now = inputs
        return (gate_now[..., None, None] * carried + state_now, carried)

    _, before = lax.scan(
        advance,
        jnp.zeros_like(local_state[:, 0]),
        (jnp.moveaxis(decay_gate, 1, 0), jnp.moveaxis(local_state, 1, 0)),
    )
    before = jnp.moveaxis(before, 0, 1)
    from_start = jnp.where((blocksegs == prev_seg[:, :, None])[..., None], jnp.exp(cumlog), 0.0)
    inter = (
        jnp.einsum("rctn,rchpn->rcthp", queries, before, precision=HIGHEST) * from_start[..., None]
    )
    scanned = (intra + inter).reshape(row_count, length, head_count, head_size) + skip_scale[
        :, None
    ] * heads_view
    return scanned.reshape(row_count, length, channels) * jax.nn.silu(z_raw)


def forward_dot(left, right):
    return jnp.dot(left, right, preferred_element_type=jnp.float32)


def inner_dot(left, right):
    return lax.dot_general(
        left, right, (((1,), (1,)), ((), ())), preferred_element_type=jnp.float32
    )


def outer_dot(left, right):
    return lax.dot_general(
        left, right, (((0,), (0,)), ((), ())), preferred_element_type=jnp.float32
    )


def shards(
    residual,
    segment_ids,
    norm_gain,
    zgate_proj,
    xin_proj,
    bc_proj,
    dt_proj,
    xconv_weight,
    xconv_bias,
    bcconv_weight,
    bcconv_bias,
    dt_bias,
    decay_log,
    skip_scale,
    gate_gain,
    out_proj,
    cotangent,
):
    row_count, share_len, model_width = residual.shape
    inv_rms = lax.rsqrt(jnp.mean(residual * residual, axis=-1, keepdims=True) + EPSILON)
    normed_low = (residual * inv_rms * norm_gain).astype(jnp.bfloat16)
    gathered = lax.all_gather(normed_low, "tensor", axis=1, tiled=True)
    length = gathered.shape[1]
    tokens_all = row_count * length
    flat_normed = gathered.reshape(tokens_all, model_width)
    z_raw = forward_dot(flat_normed, zgate_proj).reshape(row_count, length, -1)
    x_raw = forward_dot(flat_normed, xin_proj).reshape(row_count, length, -1)
    bc_raw = forward_dot(flat_normed, bc_proj).reshape(row_count, length, -1)
    dt_raw = forward_dot(flat_normed, dt_proj).reshape(row_count, length, -1)

    def local_mixer(
        x_in, bc_in, dt_in, z_in, xconv_w, xconv_b, bcconv_w, bcconv_b, dt_shift, decay_in, skip_in
    ):
        return mixer(
            x_in,
            bc_in,
            dt_in,
            z_in,
            xconv_w,
            xconv_b,
            bcconv_w,
            bcconv_b,
            dt_shift,
            decay_in,
            skip_in,
            segment_ids,
            GROUP,
        )

    gated, mixer_back = jax.vjp(
        local_mixer,
        x_raw,
        bc_raw,
        dt_raw,
        z_raw,
        xconv_weight,
        xconv_bias,
        bcconv_weight,
        bcconv_bias,
        dt_bias,
        decay_log,
        skip_scale,
    )
    square_sum = lax.psum(jnp.sum(gated * gated, axis=-1), "tensor")
    inv_gate = lax.rsqrt(square_sum / DI + EPSILON)[..., None]
    normed_gate_low = (gated * inv_gate * gate_gain).astype(jnp.bfloat16)
    flat_gate = normed_gate_low.reshape(tokens_all, -1)
    partial_out = forward_dot(flat_gate, out_proj).reshape(row_count, length, model_width)
    branch = lax.psum_scatter(partial_out, "tensor", scatter_dimension=1, tiled=True)
    block_output = residual + branch
    cot_full = lax.all_gather(cotangent.astype(jnp.bfloat16), "tensor", axis=1, tiled=True)
    cot_flat = cot_full.reshape(tokens_all, model_width)
    outproj_part = outer_dot(flat_gate, cot_flat)
    grad_normed_gate = inner_dot(cot_flat, out_proj).reshape(row_count, length, -1)
    gategain_part = jnp.sum(grad_normed_gate * gated * inv_gate, axis=(0, 1))
    scaled_gate = grad_normed_gate * gate_gain
    cross_sum = lax.psum(jnp.sum(scaled_gate * gated, axis=-1), "tensor")
    grad_gated = inv_gate * scaled_gate - gated * inv_gate**3 * (cross_sum / DI)[..., None]
    (
        grad_x,
        grad_bc_part,
        grad_dt,
        grad_z,
        xconv_part,
        xbias_part,
        bcconv_part,
        bcbias_part,
        dtbias_part,
        decay_part,
        skip_part,
    ) = mixer_back(grad_gated)
    grad_bc = lax.psum(grad_bc_part, "tensor")
    low_z = grad_z.astype(jnp.bfloat16).reshape(tokens_all, -1)
    low_x = grad_x.astype(jnp.bfloat16).reshape(tokens_all, -1)
    low_dt = grad_dt.astype(jnp.bfloat16).reshape(tokens_all, -1)
    low_bc = grad_bc.astype(jnp.bfloat16)
    grad_normed_part = (
        inner_dot(low_z, zgate_proj) + inner_dot(low_x, xin_proj) + inner_dot(low_dt, dt_proj)
    )
    grad_normed = lax.psum_scatter(
        grad_normed_part.reshape(row_count, length, model_width),
        "tensor",
        scatter_dimension=1,
        tiled=True,
    )
    own_start = lax.axis_index("tensor") * share_len
    own_bc = lax.dynamic_slice_in_dim(low_bc, own_start, share_len, 1).reshape(
        row_count * share_len, -1
    )
    grad_normed = grad_normed + inner_dot(own_bc, bc_proj).reshape(
        row_count, share_len, model_width
    )
    zproj_part = outer_dot(flat_normed, low_z)
    xproj_part = outer_dot(flat_normed, low_x)
    dtproj_part = outer_dot(flat_normed, low_dt)
    bcproj_part = outer_dot(flat_normed, low_bc.reshape(tokens_all, -1))
    scaled_in = grad_normed * norm_gain
    normgain_part = jnp.sum(grad_normed * residual * inv_rms, axis=(0, 1))
    input_grad = (
        cotangent
        + inv_rms * scaled_in
        - residual * inv_rms**3 * jnp.mean(scaled_in * residual, axis=-1, keepdims=True)
    )
    normgain_grad, bcconv_grad, bcbias_grad = lax.psum(
        (normgain_part, bcconv_part, bcbias_part), ("batch", "tensor")
    )
    (
        zproj_grad,
        xproj_grad,
        bcproj_grad,
        dtproj_grad,
        xconv_grad,
        xbias_grad,
        dtbias_grad,
        decay_grad,
        skip_grad,
        outproj_sum,
        gategain_sum,
    ) = lax.psum(
        (
            zproj_part,
            xproj_part,
            bcproj_part,
            dtproj_part,
            xconv_part,
            xbias_part,
            dtbias_part,
            decay_part,
            skip_part,
            outproj_part,
            gategain_part,
        ),
        "batch",
    )
    return (
        block_output,
        input_grad,
        normgain_grad,
        zproj_grad,
        xproj_grad,
        bcproj_grad,
        dtproj_grad,
        xconv_grad,
        xbias_grad,
        bcconv_grad,
        bcbias_grad,
        dtbias_grad,
        decay_grad,
        skip_grad,
        gategain_sum,
        outproj_sum,
    )


def solution(mesh):
    placed = (
        P("batch", "tensor", None),
        P("batch", None),
        P(),
        P(None, "tensor"),
        P(None, "tensor"),
        P(),
        P(None, "tensor"),
        P(None, "tensor"),
        P("tensor"),
        P(),
        P(),
        P("tensor"),
        P("tensor"),
        P("tensor"),
        P("tensor"),
        P("tensor", None),
        P("batch", "tensor", None),
    )
    return jax.shard_map(
        shards,
        mesh=mesh,
        in_specs=placed,
        out_specs=(
            P("batch", "tensor", None),
            P("batch", "tensor", None),
            P(),
            P(None, "tensor"),
            P(None, "tensor"),
            P(),
            P(None, "tensor"),
            P(None, "tensor"),
            P("tensor"),
            P(),
            P(),
            P("tensor"),
            P("tensor"),
            P("tensor"),
            P("tensor"),
            P("tensor", None),
        ),
        check_vma=False,
    )
```

profile of v0, /device:TPU:1, one launch (start us, length us, event | category | flops | bytes accessed | tf_op | source)
XLA Modules:
  0.0 1837.9 jit_solution(18357494443219427244)
XLA Ops:
  22.0 51.5 %all-gather.3.cloned.1.call-done = bf16[1,1024,2048]{2,1,0:T(8,128)(2,1)} async-done(((bf16[1,512,2048]{2,1,0:T(8,128)(2,1)}), bf16[1,1024,2048]{2,1,0:T(8,128)(2,1)}) %all-gather.3.cloned.1.call-update) | async-done | bytes 4194320 | tf_op jit(solution)/shard_map/all_gather | solution.py:133
  114.1 14.4 reshape.940
  128.5 14.4 reshape.937
  152.3 14.5 copy.232
  207.0 38.9 %bitcast_add_fusion.3 = f32[1,4,256,32,64]{2,4,3,1,0:T(8,128)} fusion(f32[4,256,32,64]{1,3,2,0:T(8,128)S(1)} %fusion.64, f32[4,256,32]{1,2,0:T(8,128)S(1)} %get-tuple-element.435, f32[4,256,256]{2,1,0:T(8,128)S(1)} %fusion.161, f32[4,256,32]{1,2,0:T(8,128)S(1)} %copy-done.43, pred[4,256,256]{2,1,0:T(8,128)(4,1)S(1)} %copy-done.40, ...), kind=kOutput, calls=%fused_computation.54 | convolution fusion | flops 6473908224 | bytes 26869760 | tf_op jit(solution)/shard_map/jvp(rctsh,rcshp->rcthp)/dot_general | solution.py:63
  245.9 16.2 copy.277
  262.1 14.9 reshape.938
  277.0 21.2 %multiply_reduce_fusion.8 = (f32[1024]{0:T(1024)S(1)}, f32[1024,2048]{1,0:T(8,128)}, f32[1024,2048]{1,0:T(8,128)}) fusion(f32[1024,2048]{1,0:T(8,128)} %reshape.938, f32[1,1024,2048]{2,1,0:T(8,128)} %get-tuple-element.397, f32[2048]{0:T(1024)S(1)} %mul.661, bf16[2048,2048]{1,0:T(8,128)(2,1)} %param.24, bf16[1,1024,2048]{2,1,0:T(8,128)(2,1)} %all-gather.3.cloned.1.call-done), kind=kOutput, calls=%fused_computation.81 | convolution fusion | flops 8617196544 | bytes 46149632 | tf_op jit(solution)/shard_map/dot_general | solution.py:96
  302.1 17.1 multiply_reduce_fusion
  322.9 18.3 fusion.29
  417.7 14.3 copy.258
  434.5 14.6 while.35
  449.4 48.7 %fusion.9 = (f32[4,256,32]{1,2,0:T(8,128)S(1)}, f32[4,256,32]{1,2,0:T(8,128)S(1)}, f32[4,256,256]{2,1,0:T(8,128)}) fusion(f32[4,256,32]{1,2,0:T(8,128)S(1)} %copy-done.43, f32[4,256,256]{2,1,0:T(8,128)} %copy-done.33, pred[4,256,256]{2,1,0:T(8,128)(4,1)S(1)} %copy-done.41, f32[4,256,32,64]{1,3,2,0:T(8,128)} %copy.232, f32[4,256,32]{1,2,0:T(8,128)S(1)} %bitcast.356, ...), kind=kOutput, calls=%fused_computation.22 | convolution fusion | flops 6519717888 | bytes 19660800 | tf_op jit(solution)/shard_map/transpose(jvp(rctsh,rcshp->rcthp))/dot_general | solution.py:63
  509.1 31.6 %bitcast_add_fusion.2 = f32[1,4,256,32,64]{2,4,3,1,0:T(8,128)} fusion(f32[4,32,64,256]{3,2,1,0:T(8,128)S(1)} %get-tuple-element.433, f32[4,256,32]{1,2,0:T(8,128)S(1)} %bitcast.363, f32[4,256,256]{2,1,0:T(8,128)S(1)} %copy-done.34, f32[4,256,32]{1,2,0:T(8,128)S(1)} %copy-done.44, pred[4,256,256]{2,1,0:T(8,128)(4,1)S(1)} %copy-done.41, ...), kind=kOutput, calls=%fused_computation.53 | convolution fusion | flops 6471811072 | bytes 26738688 | tf_op jit(solution)/shard_map/transpose(jvp(rctsh,rcshp->rcthp))/dot_general | solution.py:63
  553.4 16.4 copy.278
  591.1 14.8 reshape.939
  606.0 28.1 %fusion.148 = (f32[2048]{0:T(1024)}, f32[2048]{0:T(1024)}, f32[2048]{0:T(1024)}, f32[2048]{0:T(1024)}, f32[2048]{0:T(1024)}, /*index=5*/f32[1,1024,2048]{2,1,0:T(8,128)S(1)}) fusion(f32[1024,2048]{1,0:T(8,128)} %copy-done.1, f32[1,1024,2048]{2,1,0:T(8,128)} %bitcast.329, pred[1024]{0:T(1024)(128)(4,1)S(1)} %copy-done.59, pred[1024]{0:T(1024)(128)(4,1)S(1)} %copy-done.57, ...), kind=kLoop, calls=%fused_computation.250 | loop fusion | flops 50321408 | bytes 58772480 | tf_op jit(solution)/shard_map/transpose(jvp())/reduce_sum | solution.py:15
  656.3 15.1 fusion.54
  688.9 15.8 convolution_bitcast_fusion
  722.0 18.1 fusion.99
  745.5 50.8 %all-reduce.34 = bf16[1,1024,256]{2,1,0:T(8,128)(2,1)S(1)} all-reduce(f32[1,1024,256]{2,1,0:T(8,128)S(1)} %fusion.120), channel_id=1, replica_groups=mesh['batch'=16,'tensor'=2] {'tensor'}, use_global_device_ids=true, to_apply=%region_23.24 | all-reduce | flops 262144 | bytes 1572864 | tf_op jit(solution)/shard_map/psum | solution.py:203
  838.5 57.4 %all-reduce.28 = (f32[4,2048]{1,0:T(4,128)}, f32[2048]{0:T(1024)}, f32[32]{0:T(128)}, f32[32]{0:T(128)}, f32[32]{0:T(128)}, /*index=5*/f32[2048]{0:T(1024)}) all-reduce(f32[4,2048]{1,0:T(4,128)S(1)} %pad_add_fusion, f32[2048]{0:T(1024)S(1)} %copy-done.68, f32[32]{0:T(128)S(1)} %copy-done.99, ...), channel_id=1, replica_groups=mesh['batch'=16,'tensor'=2] {'batch'}, use_global_device_ids=true, to_apply=%region_35.36 | all-reduce | flops 12384 | bytes 99072 | tf_op jit(solution)/shard_map/psum | solution.py:250
  902.8 43.3 %all-reduce.27 = (f32[2048]{0:T(1024)}, f32[4,256]{1,0:T(4,128)}, f32[256]{0:T(256)}) all-reduce(f32[2048]{0:T(1024)S(1)} %get-tuple-element.331, f32[4,256]{1,0:T(4,128)S(1)} %pad_add_fusion.1, f32[256]{0:T(256)S(1)} %get-tuple-element.336), channel_id=1, replica_groups=mesh['batch'=16,'tensor'=2] {'batch','tensor'}, use_global_device_ids=true, to_apply=%region_26.27 | all-reduce | flops 3328 | bytes 26624 | tf_op jit(solution)/shard_map/psum | solution.py:235
  956.5 839.3 %all-reduce.33.cloned.1.call-done = (f32[2048,2048]{1,0:T(8,128)}, f32[2048,2048]{1,0:T(8,128)}, f32[2048,256]{1,0:T(8,128)}, f32[2048,32]{0,1:T(8,128)}, f32[2048,2048]{1,0:T(8,128)}) async-done(((f32[2048,2048]{1,0:T(8,128)}, f32[2048,2048]{1,0:T(8,128)}, f32[2048,256]{1,0:T(8,128)}, f32[2048,32]{0,1:T(8,128)}, f32[2048,2048]{1,0:T(8,128)}), (f32[2048,2048]{1,0:T(8,128)}, f32[2048,2048]{1,0:T(8,128)}, ...) | async-done | bytes 52690960 | tf_op jit(solution)/shard_map/psum | solution.py:250
  (404 shorter events, 418.9 us)
Async XLA Ops:
  7.2 138.2 %copy-start = (bf16[2048,256]{1,0:T(8,128)(2,1)S(1)}, bf16[2048,256]{1,0:T(8,128)(2,1)}, u32[]{:S(2)}) copy-start(bf16[2048,256]{1,0:T(8,128)(2,1)} %param.26) | copy-start | bytes 3145732
  7.2 66.3 %all-gather.3.cloned.1.call-start = ((), (), s32[]{:S(2)}) async-start(), calls=%async_computation.2 | async-start | bytes 6291456 | tf_op jit(solution)/shard_map/all_gather | solution.py:133
  14.5 287.5 %all-gather.5.cloned.1.call-start = ((), (), s32[]{:S(2)}) async-start(), calls=%async_computation.4 | async-start | bytes 6291456 | tf_op jit(solution)/shard_map/all_gather | solution.py:182
  18.5 877.4 %reduce-scatter.5.cloned.1.call-start = ((), (), s32[]{:S(2)}) async-start(), calls=%async_computation.5 | async-start | bytes 12582912 | tf_op jit(solution)/shard_map/reduce_scatter | solution.py:211
  18.6 75.6 %copy-start.95 = (f32[32]{0:T(128)}, f32[32]{0:T(128)S(1)}, u32[]{:S(2)}) copy-start(f32[32]{0:T(128)S(1)} %exponential_negate_fusion) | copy-start | bytes 388
  18.8 130.1 %copy-start.56 = (pred[1024]{0:T(1024)(128)(4,1)}, pred[1024]{0:T(1024)(128)(4,1)S(1)}, u32[]{:S(2)}) copy-start(pred[1024]{0:T(1024)(128)(4,1)S(1)} %get-tuple-element.343) | copy-start | bytes 3076
  18.8 130.1 %copy-start.58 = (pred[1024]{0:T(1024)(128)(4,1)}, pred[1024]{0:T(1024)(128)(4,1)S(1)}, u32[]{:S(2)}) copy-start(pred[1024]{0:T(1024)(128)(4,1)S(1)} %get-tuple-element.344) | copy-start | bytes 3076
  18.8 130.1 %copy-start.60 = (pred[1024]{0:T(1024)(128)(4,1)}, pred[1024]{0:T(1024)(128)(4,1)S(1)}, u32[]{:S(2)}) copy-start(pred[1024]{0:T(1024)(128)(4,1)S(1)} %get-tuple-element.345) | copy-start | bytes 3076
  20.6 146.2 %copy-start.93 = (pred[4]{0:T(512)(128)(4,1)}, pred[4]{0:T(512)(128)(4,1)S(1)}, u32[]{:S(2)}) copy-start(pred[4]{0:T(512)(128)(4,1)S(1)} %compare_reduce_fusion.3) | copy-start | bytes 16
  20.6 128.3 %copy-start.82 = (f32[1,256]{1,0:T(1,128)}, f32[1,256]{1,0:T(1,128)S(1)}, u32[]{:S(2)}) copy-start(f32[1,256]{1,0:T(1,128)S(1)} %get-tuple-element.422) | copy-start | bytes 3076
  20.6 128.3 %copy-start.84 = (f32[1,256]{1,0:T(1,128)}, f32[1,256]{1,0:T(1,128)S(1)}, u32[]{:S(2)}) copy-start(f32[1,256]{1,0:T(1,128)S(1)} %get-tuple-element.423) | copy-start | bytes 3076
  20.6 128.3 %copy-start.86 = (f32[1,256]{1,0:T(1,128)}, f32[1,256]{1,0:T(1,128)S(1)}, u32[]{:S(2)}) copy-start(f32[1,256]{1,0:T(1,128)S(1)} %get-tuple-element.424) | copy-start | bytes 3076
  20.6 128.3 %copy-start.88 = (f32[1,256]{1,0:T(1,128)}, f32[1,256]{1,0:T(1,128)S(1)}, u32[]{:S(2)}) copy-start(f32[1,256]{1,0:T(1,128)S(1)} %get-tuple-element.421) | copy-start | bytes 3076
  20.8 73.5 %copy-start.46 = (f32[1,2048]{1,0:T(1,128)}, f32[1,2048]{1,0:T(1,128)S(1)}, u32[]{:S(2)}) copy-start(f32[1,2048]{1,0:T(1,128)S(1)} %get-tuple-element.415) | copy-start | bytes 24580
  20.8 73.5 %copy-start.48 = (f32[1,2048]{1,0:T(1,128)}, f32[1,2048]{1,0:T(1,128)S(1)}, u32[]{:S(2)}) copy-start(f32[1,2048]{1,0:T(1,128)S(1)} %get-tuple-element.416) | copy-start | bytes 24580
  20.8 73.5 %copy-start.50 = (f32[1,2048]{1,0:T(1,128)}, f32[1,2048]{1,0:T(1,128)S(1)}, u32[]{:S(2)}) copy-start(f32[1,2048]{1,0:T(1,128)S(1)} %get-tuple-element.417) | copy-start | bytes 24580
  20.9 73.5 %copy-start.52 = (f32[1,2048]{1,0:T(1,128)}, f32[1,2048]{1,0:T(1,128)S(1)}, u32[]{:S(2)}) copy-start(f32[1,2048]{1,0:T(1,128)S(1)} %get-tuple-element.418) | copy-start | bytes 24580
  21.0 122.4 %copy-start.80 = (pred[4,256]{1,0:T(4,128)(4,1)}, pred[4,256]{1,0:T(4,128)(4,1)S(1)}, u32[]{:S(2)}) copy-start(pred[4,256]{1,0:T(4,128)(4,1)S(1)} %get-tuple-element.420) | copy-start | bytes 3076
  21.0 123.4 %copy-start.78 = (pred[4,256]{1,0:T(4,128)(4,1)}, pred[4,256]{1,0:T(4,128)(4,1)S(1)}, u32[]{:S(2)}) copy-start(pred[4,256]{1,0:T(4,128)(4,1)S(1)} %get-tuple-element.419) | copy-start | bytes 3076
  145.4 249.3 %copy-start.31 = (f32[4,256,32]{1,2,0:T(8,128)}, f32[4,256,32]{1,2,0:T(8,128)S(1)}, u32[]{:S(2)}) copy-start(f32[4,256,32]{1,2,0:T(8,128)S(1)} %get-tuple-element.435) | copy-start | bytes 393220
  152.3 242.4 %copy-start.16 = (f32[1,1024,128]{2,1,0:T(8,128)}, f32[1,1024,128]{2,1,0:T(8,128)S(1)}, u32[]{:S(2)}) copy-start(f32[1,1024,128]{2,1,0:T(8,128)S(1)} %get-tuple-element.411) | copy-start | bytes 1572868
  688.2 258.0 %reduce-scatter.3.cloned.1.call-start = ((), (), s32[]{:S(2)}) async-start(), calls=%async_computation.3 | async-start | bytes 12582912 | tf_op jit(solution)/shard_map/reduce_scatter | solution.py:180
  704.8 1091.1 %all-reduce.33.cloned.1.call-start = ((), (), s32[]{:S(2)}) async-start(), calls=%async_computation.6 | async-start | bytes 105381888 | tf_op jit(solution)/shard_map/psum | solution.py:250
  837.6 108.6 %copy-start.91 = (f32[512]{0:T(512)S(1)}, f32[512]{0:T(512)}, u32[]{:S(2)}) copy-start(f32[512]{0:T(512)} %get-tuple-element.425) | copy-start | bytes 6148
  (98 other events, 1568.4 us)
Sparse Core Ops, SparseCore 0:
  14.7 58.7 all-gather.2
  75.1 56.7 all-gather.4
  688.3 124.0 reduce-scatter.4
  814.6 99.4 reduce-scatter.2
  920.4 875.3 all-reduce.32
where the time goes:
time: 1840 us
  waiting for transfers between devices  891 us (48%)
  matrix products  358 us (19%)
  local copies, waits for them, and re-layouts  240 us (13%)
  other arithmetic  174 us (9%)
  blocking collectives  159 us (9%)
    psum x1, waiting for transfers between devices, shards(): lax.psum((zproj_part, xproj_part, bcproj_part, dtproj_part, xconv_part, x...  839 us
    dot_general x3, matrix products, mixer(): intra = jnp.einsum('rctsh,rcshp->rcthp', mixing, values, precision=HIGHEST)  119 us
    dot_general x5, matrix products, inner_dot(): lax.dot_general(left, right, (((1,), (1,)), ((), ())), preferred_element_...  62.6 us
    dot_general x5, matrix products, forward_dot(): return jnp.dot(left, right, preferred_element_type=jnp.float32)  58.3 us
    reshape x4, local copies, waits for them, and re-layouts, mixer(): heads_view = xconv.reshape(row_count, length, head_count, head_size)  57.6 us
    psum x1, blocking collectives, shards(): lax.psum((zproj_part, xproj_part, bcproj_part, dtproj_part, xconv_part, x...  57.4 us
    reshape x4, local copies, waits for them, and re-layouts, mixer(): (intra + inter).reshape(row_count, length, head_count, head_size)  52.2 us
    all_gather x1, waiting for transfers between devices, shards(): gathered = lax.all_gather(normed_low, 'tensor', axis=1, tiled=True)  51.5 us
  transfers between devices with their start and end apart: 5, of which 2 were waited for; matrix products, arithmetic and copies ran while one was open for 19% of the time, Pallas kernels for 0%

commit v1 on v0

v1 whole, which is shorter than its diff:
```python
import functools
import jax
import jax.numpy as jnp
from jax import lax
from jax.experimental import pallas as pl
from jax.experimental.pallas import tpu as pltpu
from jax.sharding import Mesh, PartitionSpec as P

EPSILON = 1e-05
BLOCK = 128
LANES = 128
BF = jnp.bfloat16
F32 = jnp.float32
NEG = -1e30
VMEM_LIMIT = 56 * 1024 * 1024


def dot(a, b):
    return jnp.dot(a, b, preferred_element_type=F32)


def dot_nt(a, b):
    return lax.dot_general(a, b, (((1,), (1,)), ((), ())), preferred_element_type=F32)


def dot_tn(a, b):
    return lax.dot_general(a, b, (((0,), (0,)), ((), ())), preferred_element_type=F32)


def dot_exact(a, b):
    return jnp.dot(a, b, precision=lax.Precision.HIGHEST, preferred_element_type=F32)


def iota(shape, dim):
    return lax.broadcasted_iota(jnp.int32, shape, dim)


def sigmoid(v):
    return 1.0 / (1.0 + jnp.exp(-v))


def conv_terms(prev, cur, masks):
    window = jnp.concatenate([prev, cur], axis=0)
    rows = cur.shape[0]
    return [cur] + [masks[k - 1] * window[8 - k : 8 - k + rows] for k in (1, 2, 3)]


def conv_sum(terms, prm):
    total = prm[4:5] + prm[0:1] * terms[0]
    for k in (1, 2, 3):
        total = total + prm[k : k + 1] * terms[k]
    return total


def conv_masks(meta):
    return [meta[:, k : k + 1] for k in (0, 1, 2)]


def split_three(v, heads):
    high = v.astype(BF).astype(F32)
    rest = v - high
    mid = rest.astype(BF).astype(F32)
    low = rest - mid
    return (high + pltpu.roll(mid, heads, 1) + pltpu.roll(low, 2 * heads, 1)).astype(BF)


def prep_kernel(heads, normed, wcat, meta, bcw, aux, raw_o, kq_o, kt_o, qt_o, cum_o, cumt_o, pk_o, halo):
    rows = normed.shape[0]
    state = kt_o.shape[0]

    @pl.when(pl.program_id(0) == 0)
    def _():
        halo[...] = jnp.zeros_like(halo)

    raw = dot(normed[...], wcat[...])
    bc = raw[:, : 2 * state]
    shifted_dt = raw[:, 2 * state :] + aux[0:1]
    raw_o[:, : 2 * state] = bc
    raw_o[:, 2 * state :] = shifted_dt
    m = meta[...]
    conv = conv_sum(conv_terms(halo[...], bc, conv_masks(m)), bcw[...])
    halo[...] = bc[rows - 8 :]
    act = conv * sigmoid(conv)
    kq_o[...] = act.astype(BF)
    kt_o[...] = act[:, :state].T.astype(BF)
    qt_o[...] = act[:, state:].T.astype(BF)
    real = iota((rows, LANES), 1) < heads
    step = jnp.where(
        real, jnp.maximum(shifted_dt, 0.0) + jnp.log1p(jnp.exp(-jnp.abs(shifted_dt))), 0.0
    )
    logdecay = -jnp.exp(aux[1:2]) * step
    tri = (iota((rows, rows), 0) >= iota((rows, rows), 1)).astype(F32)
    cum = dot_exact(tri, logdecay)
    cum_o[...] = cum
    cumt_o[...] = cum.T[: cumt_o.shape[0]]
    start = jnp.where(real, jnp.exp(cum) * m[:, 4:5], 0.0)
    end = jnp.where(real, jnp.exp(cum[rows - 1 :] - cum) * m[:, 5:6], 0.0)
    pk_o[0] = split_three(step, heads)
    pk_o[1] = split_three(start, heads)
    pk_o[2] = split_three(end, heads)


def prep(normed, wcat, meta, bcw, aux, heads, state):
    tokens, width = normed.shape
    hrows = max(8, -(-heads // 8) * 8)
    cols = wcat.shape[1]
    rep = lambda b: (0, 0)
    return pl.pallas_call(
        functools.partial(prep_kernel, heads),
        grid=(tokens // BLOCK,),
        in_specs=[
            pl.BlockSpec((BLOCK, width), lambda b: (b, 0)),
            pl.BlockSpec((width, cols), rep),
            pl.BlockSpec((BLOCK, LANES), lambda b: (b, 0)),
            pl.BlockSpec((8, 2 * state), rep),
            pl.BlockSpec((8, LANES), rep),
        ],
        out_specs=[
            pl.BlockSpec((BLOCK, cols), lambda b: (b, 0)),
            pl.BlockSpec((BLOCK, 2 * state), lambda b: (b, 0)),
            pl.BlockSpec((state, BLOCK), lambda b: (0, b)),
            pl.BlockSpec((state, BLOCK), lambda b: (0, b)),
            pl.BlockSpec((BLOCK, LANES), lambda b: (b, 0)),
            pl.BlockSpec((hrows, BLOCK), lambda b: (0, b)),
            pl.BlockSpec((3, BLOCK, LANES), lambda b: (0, b, 0)),
        ],
        out_shape=[
            jax.ShapeDtypeStruct((tokens, cols), F32),
            jax.ShapeDtypeStruct((tokens, 2 * state), BF),
            jax.ShapeDtypeStruct((state, tokens), BF),
            jax.ShapeDtypeStruct((state, tokens), BF),
            jax.ShapeDtypeStruct((tokens, LANES), F32),
            jax.ShapeDtypeStruct((hrows, tokens), F32),
            jax.ShapeDtypeStruct((3, tokens, LANES), BF),
        ],
        scratch_shapes=[pltpu.VMEM((8, 2 * state), F32)],
        compiler_params=pltpu.CompilerParams(
            dimension_semantics=("arbitrary",), vmem_limit_bytes=VMEM_LIMIT
        ),
        cost_estimate=pl.CostEstimate(
            flops=2 * tokens * width * cols, bytes_accessed=8 << 20, transcendentals=0
        ),
        name="prep",
    )(normed, wcat, meta, bcw, aux)


def head_spread(group, heads, head_size, width):
    r, c = iota((LANES, width), 0), iota((LANES, width), 1)
    head = (group * width + c) // head_size
    hit = (r == head) | (r == head + heads) | (r == head + 2 * heads)
    return jnp.where(hit, 1.0, 0.0).astype(BF)


def head_gather(group, head_size, width):
    c, r = iota((width, LANES), 0), iota((width, LANES), 1)
    return jnp.where(r == (group * width + c) // head_size, 1.0, 0.0).astype(BF)


def reduce_heads(v, gather):
    high = v.astype(BF)
    low = (v - high.astype(F32)).astype(BF)
    return dot(high, gather) + dot(low, gather)


def stack_pair(v, head_size):
    first = iota(v.shape, 1) < head_size
    zero = jnp.zeros_like(v)
    return jnp.concatenate([jnp.where(first, v, zero), jnp.where(first, zero, v)], axis=0)


def fwd_kernel(heads, head_size, state, x, z, meta, segrow, kq, kt, cum, cumt, pk, prm,
               scan_o, before_o, square_o, carried, spread):
    group = pl.program_id(0)
    tokens, width = x.shape
    per_group = width // head_size
    spread[...] = head_spread(group, heads, head_size, width)
    carried[...] = jnp.zeros_like(carried)

    @pl.when(group == 0)
    def _():
        square_o[...] = jnp.zeros_like(square_o)

    p = prm[...]

    @pl.loop(0, tokens // BLOCK)
    def _(b):
        start = pl.multiple_of(b * BLOCK, BLOCK)
        rows = pl.ds(start, BLOCK)
        prev_rows = pl.ds(pl.multiple_of(jnp.maximum(start - 8, 0), 8), 8)
        m = meta[rows]
        masks = conv_masks(m)
        keys, queries = kq[rows, :state], kq[rows, state:]
        scores = dot_nt(queries, keys)
        causal = iota((BLOCK, BLOCK), 0) >= iota((BLOCK, BLOCK), 1)
        shut = jnp.where((m[:, 3:4] == segrow[0:1, rows]) & causal, 0.0, NEG)
        cum_rows = pltpu.roll(cum[rows], lax.rem(LANES - group * per_group, LANES), 1)
        cum_cols = cumt[pl.ds(pl.multiple_of(group * per_group, per_group), per_group), rows]
        step_b = dot(pk[0, rows], spread[...])
        start_b = dot(pk[1, rows], spread[...])
        end_b = dot(pk[2, rows], spread[...])
        old = carried[...]
        before_o[b] = old.astype(BF)
        inter = dot(queries, old.astype(BF)) * start_b
        weighted = []
        square = jnp.zeros((BLOCK, LANES), F32)
        for j in range(width // LANES):
            at = slice(j * LANES, (j + 1) * LANES)
            conv = conv_sum(conv_terms(x[prev_rows, at], x[rows, at], masks), p[:, at])
            xs = conv * sigmoid(conv)
            values = xs * step_b[:, at]
            weighted.append((values * end_b[:, at]).astype(BF))
            pair = stack_pair(values.astype(BF), head_size)
            mixing = []
            for h in range(j * LANES // head_size, (j + 1) * LANES // head_size):
                decay = jnp.exp((cum_rows[:, h : h + 1] - cum_cols[h : h + 1]) + shut)
                mixing.append((decay * scores).astype(BF))
            intra = dot(jnp.concatenate(mixing, axis=1), pair)
            scan = intra + inter[:, at] + p[5:6, at] * xs
            scan_o[rows, at] = scan
            gate = z[rows, at]
            gated = scan * (gate * sigmoid(gate))
            square = square + gated * gated
        square_o[rows] = square_o[rows] + square
        carried[...] = start_b[BLOCK - 1 :] * old + dot(kt[:, rows], jnp.concatenate(weighted, axis=1))


def fwd(x, z, meta, segrow, kq, kt, cum, cumt, pk, prm, heads, head_size, state, width):
    tokens, channels = x.shape
    blocks = tokens // BLOCK
    whole = lambda a: pl.BlockSpec(a.shape, lambda g, n=a.ndim: (0,) * n)
    col = lambda rows: pl.BlockSpec((rows, width), lambda g: (0, g))
    return pl.pallas_call(
        functools.partial(fwd_kernel, heads, head_size, state),
        grid=(channels // width,),
        in_specs=[col(tokens), col(tokens), whole(meta), whole(segrow), whole(kq), whole(kt),
                  whole(cum), whole(cumt), whole(pk), col(8)],
        out_specs=[
            col(tokens),
            pl.BlockSpec((blocks, state, width), lambda g: (0, 0, g)),
            pl.BlockSpec((tokens, LANES), lambda g: (0, 0)),
        ],
        out_shape=[
            jax.ShapeDtypeStruct((tokens, channels), F32),
            jax.ShapeDtypeStruct((blocks, state, channels), BF),
            jax.ShapeDtypeStruct((tokens, LANES), F32),
        ],
        scratch_shapes=[pltpu.VMEM((state, width), F32), pltpu.VMEM((LANES, width), BF)],
        compiler_params=pltpu.CompilerParams(
            dimension_semantics=("arbitrary",), vmem_limit_bytes=VMEM_LIMIT
        ),
        cost_estimate=pl.CostEstimate(
            flops=20 * 1024 * 1024 * 1024, bytes_accessed=32 << 20, transcendentals=0
        ),
        name="scan_forward",
    )(x, z, meta, segrow, kq, kt, cum, cumt, pk, prm)


def bwd_kernel(heads, head_size, state, first_group, x, dy, scan, before, meta, segrow, kq, qt, cum,
               cumt, pk, prm, low_o, dkq_o, dc_o, ds_o, pg_o, carried, spread, gather, later):
    local = pl.program_id(0)
    group = local + first_group
    tokens, width = x.shape
    per_group = width // head_size
    blocks = tokens // BLOCK
    spread[...] = head_spread(group, heads, head_size, width)
    gather[...] = head_gather(group, head_size, width)
    carried[...] = jnp.zeros_like(carried)
    later[...] = jnp.zeros_like(later)
    pg_o[...] = jnp.zeros_like(pg_o)

    @pl.when(local == 0)
    def _():
        dkq_o[...] = jnp.zeros_like(dkq_o)
        dc_o[...] = jnp.zeros_like(dc_o)
        ds_o[...] = jnp.zeros_like(ds_o)

    p = prm[...]

    @pl.loop(0, blocks)
    def _(i):
        b = blocks - 1 - i
        start = pl.multiple_of(b * BLOCK, BLOCK)
        rows = pl.ds(start, BLOCK)
        prev_rows = pl.ds(pl.multiple_of(jnp.maximum(start - 8, 0), 8), 8)
        m = meta[rows]
        masks = conv_masks(m)
        keys, queries = kq[rows, :state], kq[rows, state:]
        scores = dot_nt(keys, queries)
        causal = iota((BLOCK, BLOCK), 0) <= iota((BLOCK, BLOCK), 1)
        shut = jnp.where((m[:, 3:4] == segrow[0:1, rows]) & causal, 0.0, NEG)
        cum_rows = pltpu.roll(cum[rows], lax.rem(LANES - group * per_group, LANES), 1)
        cum_cols = cumt[pl.ds(pl.multiple_of(group * per_group, per_group), per_group), rows]
        step_b = dot(pk[0, rows], spread[...])
        start_b = dot(pk[1, rows], spread[...])
        end_b = dot(pk[2, rows], spread[...])
        ahead = carried[...]
        ahead_low = ahead.astype(BF)
        old = before[b]
        from_state = dot(keys, ahead_low) * end_b
        carry_grad = jnp.sum(old.astype(F32) * ahead, axis=0, keepdims=True) * start_b[BLOCK - 1 :]
        dscores = jnp.zeros((BLOCK, BLOCK), F32)
        weighted, incoming, flow, steps, ends = [], [], [], [], []
        for j in range(width // LANES):
            at = slice(j * LANES, (j + 1) * LANES)
            terms = conv_terms(x[prev_rows, at], x[rows, at], masks)
            conv = conv_sum(terms, p[:, at])
            sig = sigmoid(conv)
            xs = conv * sig
            values = xs * step_b[:, at]
            weighted.append((values * end_b[:, at]).astype(BF))
            values_low = values.astype(BF)
            dy_low = dy[rows, at]
            dy_j = dy_low.astype(F32)
            incoming.append((dy_j * start_b[:, at]).astype(BF))
            outer = dot_nt(stack_pair(values_low, head_size), dy_low)
            mixing = []
            for k, h in enumerate(range(j * LANES // head_size, (j + 1) * LANES // head_size)):
                decay = jnp.exp((cum_cols[h : h + 1] - cum_rows[:, h : h + 1]) + shut)
                mixing.append((decay * scores).astype(BF))
                dscores = dscores + decay * outer[k * BLOCK : (k + 1) * BLOCK]
            dvalues = dot(jnp.concatenate(mixing, axis=1), stack_pair(dy_low, head_size))
            late = from_state[:, at]
            skip = p[5:6, at]
            values_f = values_low.astype(F32)
            total = dvalues + late
            flow.append(dy_j * (scan[rows, at] - skip * xs) - values_f * total)
            ends.append(jnp.sum(values_f * late, axis=0, keepdims=True))
            steps.append(xs * total)
            dxs = step_b[:, at] * total + skip * dy_j
            dconv = dxs * (sig * (1.0 + conv * (1.0 - sig)))
            sums = [jnp.sum(dconv * t, axis=0, keepdims=True) for t in terms]
            sums.append(jnp.sum(dconv, axis=0, keepdims=True))
            sums.append(jnp.sum(dy_j * xs, axis=0, keepdims=True))
            sums.append(jnp.zeros((2, LANES), F32))
            pg_o[:, at] = pg_o[:, at] + jnp.concatenate(sums, axis=0)
            grad = p[0:1, at] * dconv
            for k in (1, 2, 3):
                masked = masks[k - 1] * dconv
                window = jnp.concatenate([masked, later[k - 1, :, at]], axis=0)
                grad = grad + p[k : k + 1, at] * window[k : k + BLOCK]
                later[k - 1, :, at] = masked[:8]
            low_o[rows, at] = grad.astype(BF)
        weighted = jnp.concatenate(weighted, axis=1)
        incoming = jnp.concatenate(incoming, axis=1)
        closing = carry_grad + jnp.concatenate(ends, axis=1)
        flow = jnp.concatenate(flow, axis=1)
        steps = jnp.concatenate(steps, axis=1)
        last = iota((BLOCK, width), 0) == BLOCK - 1
        flow = flow + jnp.where(last, closing, 0.0)
        dc_o[rows] = dc_o[rows] + reduce_heads(flow, gather[...])
        ds_o[rows] = ds_o[rows] + reduce_heads(steps, gather[...])
        dscores_low = dscores.astype(BF)
        dkq_o[rows, :state] = dkq_o[rows, :state] + (
            dot(dscores_low, queries) + dot_nt(weighted, ahead_low)
        )
        dkq_o[rows, state:] = dkq_o[rows, state:] + (
            dot_tn(dscores_low, keys) + dot_nt(incoming, old)
        )
        carried[...] = start_b[BLOCK - 1 :] * ahead + dot(qt[:, rows], incoming)


def bwd(x, dy, scan, before, meta, segrow, kq, qt, cum, cumt, pk, prm, heads, head_size, state, width,
        first_group, groups):
    tokens, channels = x.shape
    blocks = tokens // BLOCK
    whole = lambda a: pl.BlockSpec(a.shape, lambda g, n=a.ndim: (0,) * n)
    col = lambda rows: pl.BlockSpec((rows, width), lambda g: (0, g + first_group))
    out_col = lambda rows: pl.BlockSpec((rows, width), lambda g: (0, g))
    same = lambda g: (0, 0)
    return pl.pallas_call(
        functools.partial(bwd_kernel, heads, head_size, state, first_group),
        grid=(groups,),
        in_specs=[col(tokens), col(tokens), col(tokens),
                  pl.BlockSpec((blocks, state, width), lambda g: (0, 0, g + first_group)),
                  whole(meta), whole(segrow), whole(kq), whole(qt), whole(cum), whole(cumt), whole(pk),
                  col(8)],
        out_specs=[
            out_col(tokens),
            pl.BlockSpec((tokens, 2 * state), same),
            pl.BlockSpec((tokens, LANES), same),
            pl.BlockSpec((tokens, LANES), same),
            out_col(8),
        ],
        out_shape=[
            jax.ShapeDtypeStruct((tokens, groups * width), BF),
            jax.ShapeDtypeStruct((tokens, 2 * state), F32),
            jax.ShapeDtypeStruct((tokens, LANES), F32),
            jax.ShapeDtypeStruct((tokens, LANES), F32),
            jax.ShapeDtypeStruct((8, groups * width), F32),
        ],
        scratch_shapes=[
            pltpu.VMEM((state, width), F32),
            pltpu.VMEM((LANES, width), BF),
            pltpu.VMEM((width, LANES), BF),
            pltpu.VMEM((3, 8, width), F32),
        ],
        compiler_params=pltpu.CompilerParams(
            dimension_semantics=("arbitrary",), vmem_limit_bytes=VMEM_LIMIT
        ),
        cost_estimate=pl.CostEstimate(
            flops=groups * 10 * 1024 * 1024 * 1024, bytes_accessed=groups * (8 << 20), transcendentals=0
        ),
        name="scan_backward",
    )(x, dy, scan, before, meta, segrow, kq, qt, cum, cumt, pk, prm)


def post_kernel(heads, parts, raw, meta, bcw, aux, *refs):
    dkqs, dcs, dss = refs[:parts], refs[parts : 2 * parts], refs[2 * parts : 3 * parts]
    low_o, bg_o, dg_o, later = refs[3 * parts :]
    state2 = bcw.shape[1]
    tokens = raw.shape[0]
    blocks = tokens // BLOCK
    later[...] = jnp.zeros_like(later)
    bg_o[...] = jnp.zeros_like(bg_o)
    dg_o[...] = jnp.zeros_like(dg_o)
    w = bcw[...]
    rate = jnp.exp(aux[1:2])
    real = iota((BLOCK, LANES), 1) < heads

    @pl.loop(0, blocks)
    def _(i):
        b = blocks - 1 - i
        start = pl.multiple_of(b * BLOCK, BLOCK)
        rows = pl.ds(start, BLOCK)
        prev_rows = pl.ds(pl.multiple_of(jnp.maximum(start - 8, 0), 8), 8)
        masks = conv_masks(meta[rows])
        terms = conv_terms(raw[prev_rows, :state2], raw[rows, :state2], masks)
        conv = conv_sum(terms, w)
        sig = sigmoid(conv)
        dact = dkqs[0][rows]
        for r in dkqs[1:]:
            dact = dact + r[rows]
        dconv = dact * (sig * (1.0 + conv * (1.0 - sig)))
        sums = [jnp.sum(dconv * t, axis=0, keepdims=True) for t in terms]
        sums.append(jnp.sum(dconv, axis=0, keepdims=True))
        sums.append(jnp.zeros((3, state2), F32))
        bg_o[...] = bg_o[...] + jnp.concatenate(sums, axis=0)
        grad = w[0:1] * dconv
        for k in (1, 2, 3):
            masked = masks[k - 1] * dconv
            window = jnp.concatenate([masked, later[k - 1]], axis=0)
            grad = grad + w[k : k + 1] * window[k : k + BLOCK]
            later[k - 1] = masked[:8]
        low_o[rows, :state2] = grad.astype(BF)
        flow, direct = dcs[0][rows], dss[0][rows]
        for r in dcs[1:]:
            flow = flow + r[rows]
        for r in dss[1:]:
            direct = direct + r[rows]
        shifted_dt = raw[rows, state2:]
        step = jnp.maximum(shifted_dt, 0.0) + jnp.log1p(jnp.exp(-jnp.abs(shifted_dt)))
        tri = (iota((BLOCK, BLOCK), 0) <= iota((BLOCK, BLOCK), 1)).astype(F32)
        dlog = dot_exact(tri, flow)
        decay_sum = jnp.sum(jnp.where(real, dlog * (-rate * step), 0.0), axis=0, keepdims=True)
        grad_dt = jnp.where(real, (direct - rate * dlog) * sigmoid(shifted_dt), 0.0)
        low_o[rows, state2:] = grad_dt.astype(BF)
        dg_o[...] = dg_o[...] + jnp.concatenate(
            [jnp.sum(grad_dt, axis=0, keepdims=True), decay_sum, jnp.zeros((6, LANES), F32)], axis=0
        )


def post(raw, meta, bcw, aux, dkqs, dcs, dss, heads):
    tokens, cols = raw.shape
    return pl.pallas_call(
        functools.partial(post_kernel, heads, len(dkqs)),
        out_shape=[
            jax.ShapeDtypeStruct((tokens, cols), BF),
            jax.ShapeDtypeStruct((8, bcw.shape[1]), F32),
            jax.ShapeDtypeStruct((8, LANES), F32),
        ],
        scratch_shapes=[pltpu.VMEM((3, 8, bcw.shape[1]), F32)],
        compiler_params=pltpu.CompilerParams(vmem_limit_bytes=VMEM_LIMIT),
        cost_estimate=pl.CostEstimate(flops=1 << 32, bytes_accessed=16 << 20, transcendentals=0),
        name="post",
    )(raw, meta, bcw, aux, *dkqs, *dcs, *dss)


def position_facts(segments):
    row_count, length = segments.shape
    docs = (segments + 1024 * lax.broadcasted_iota(jnp.int32, segments.shape, 0)).reshape(-1)
    tokens = docs.shape[0]
    cols = []
    for k in (1, 2, 3):
        earlier = jnp.concatenate([jnp.full((k,), -1, jnp.int32), docs[:-k]])
        cols.append(earlier == docs)
    tiles = docs.reshape(tokens // BLOCK, BLOCK)
    last = tiles[:, -1:]
    prev = jnp.concatenate([jnp.full((1, 1), -1, jnp.int32), last[:-1]], axis=0)
    cols.append(docs)
    cols.append((tiles == prev).reshape(-1))
    cols.append((tiles == last).reshape(-1))
    lane = lax.broadcasted_iota(jnp.int32, (tokens, LANES), 1)
    meta = jnp.zeros((tokens, LANES), F32)
    for i, c in enumerate(cols):
        meta = jnp.where(lane == i, c.astype(F32)[:, None], meta)
    segrow = jnp.broadcast_to(docs.astype(F32)[None], (8, tokens))
    return meta, segrow


def shards(tensor_count, residual, segment_ids, norm_gain, zgate_proj, xin_proj, bc_proj, dt_proj,
           xconv_weight, xconv_bias, bcconv_weight, bcconv_bias, dt_bias, decay_log, skip_scale,
           gate_gain, out_proj, cotangent):
    row_count, share_len, model_width = residual.shape
    channels, heads = zgate_proj.shape[1], dt_proj.shape[1]
    head_size = channels // heads
    state = bc_proj.shape[1] // 2
    inner = channels * tensor_count
    width = min(512, channels)
    groups = channels // width
    every = ("z", "x", "core")

    inv_rms = lax.rsqrt(jnp.mean(residual * residual, axis=-1, keepdims=True) + EPSILON)
    normed_low = (residual * inv_rms * norm_gain).astype(BF)
    gathered = lax.all_gather(normed_low, "tensor", axis=1, tiled=True)
    length = gathered.shape[1]
    tokens = row_count * length
    normed = gathered.reshape(tokens, model_width)
    cot_low = cotangent.astype(BF)
    cot = lax.all_gather(cot_low, "tensor", axis=1, tiled=True).reshape(tokens, model_width)

    meta, segrow = position_facts(segment_ids)
    wcat = jnp.concatenate([bc_proj, jnp.pad(dt_proj, ((0, 0), (0, LANES - heads)))], axis=1)
    bcw = jnp.concatenate([bcconv_weight, bcconv_bias[None], jnp.zeros((3, 2 * state), F32)], axis=0)
    aux = jnp.pad(jnp.stack([dt_bias, decay_log]), ((0, 6), (0, LANES - heads)))
    prm = jnp.concatenate(
        [xconv_weight, xconv_bias[None], jnp.repeat(skip_scale, head_size)[None],
         jnp.zeros((2, channels), F32)], axis=0)

    z_raw = dot(normed, zgate_proj)
    x_raw = dot(normed, xin_proj)
    raw, kq, kt, qt, cum, cumt, pk = prep(normed, wcat, meta, bcw, aux, heads, state)
    scan, before, square = fwd(
        x_raw, z_raw, meta, segrow, kq, kt, cum, cumt, pk, prm, heads, head_size, state, width)
    grad_normed_gate = dot_nt(cot, out_proj)
    gate_sig = jax.nn.sigmoid(z_raw)
    gate_act = z_raw * gate_sig
    gated = scan * gate_act
    scaled = grad_normed_gate * gate_gain
    stats = lax.psum(
        jnp.stack([jnp.sum(square, axis=-1), jnp.sum(scaled * gated, axis=-1)]), "tensor")
    inv_gate = lax.rsqrt(stats[0] / inner + EPSILON)[:, None]
    pull = inv_gate**3 * (stats[1] / inner)[:, None]
    gate_low = (gated * inv_gate * gate_gain).astype(BF)
    gategain_part = jnp.sum(grad_normed_gate * gated * inv_gate, axis=0)
    grad_gated = inv_gate * scaled - gated * pull
    low_z = (grad_gated * scan * (gate_sig * (1.0 + z_raw * (1.0 - gate_sig)))).astype(BF)
    dy = (grad_gated * gate_act).astype(BF)

    outproj_part = dot_tn(gate_low, cot).astype(BF)
    outproj_grad = lax.psum(outproj_part, every).astype(F32)
    zproj_part = dot_tn(normed, low_z).astype(BF)
    zproj_grad = lax.psum(zproj_part, every).astype(F32)

    partial_out = dot(gate_low, out_proj).astype(BF).reshape(row_count, length, model_width)
    branch = lax.psum_scatter(partial_out, "tensor", scatter_dimension=1, tiled=True)
    block_output = residual + branch.astype(F32)

    low_x, dkq, dc, ds, pg = bwd(
        x_raw, dy, scan, before, meta, segrow, kq, qt, cum, cumt, pk, prm, heads, head_size, state,
        width, 0, groups)
    xproj_part = dot_tn(normed, low_x).astype(BF)
    xproj_grad = lax.psum(xproj_part, every).astype(F32)
    low_small, bg, dg = post(raw, meta, bcw, aux, [dkq], [dc], [ds], heads)
    small_part = dot_tn(low_small, normed)

    grad_part = dot_nt(low_z, zgate_proj) + dot_nt(low_x, xin_proj) + dot_nt(low_small, wcat)
    grad_normed = lax.psum_scatter(
        grad_part.astype(BF).reshape(row_count, length, model_width), "tensor", scatter_dimension=1,
        tiled=True).astype(F32)
    scaled_in = grad_normed * norm_gain
    normgain_part = jnp.sum(grad_normed * residual * inv_rms, axis=(0, 1))
    input_grad = (
        cotangent + inv_rms * scaled_in
        - residual * inv_rms**3 * jnp.mean(scaled_in * residual, axis=-1, keepdims=True))

    skip_part = jnp.sum(pg[5].reshape(heads, head_size), axis=-1)
    bcproj_t, bg, normgain_grad = lax.psum(
        (small_part[: 2 * state], bg, normgain_part), every + ("tensor",))
    dtproj_t, pg, dg, gategain_grad, skip_grad = lax.psum(
        (small_part[2 * state : 2 * state + heads], pg[:5], dg[:2, :heads], gategain_part, skip_part),
        every)
    return (
        block_output, input_grad, normgain_grad, zproj_grad, xproj_grad, bcproj_t.T, dtproj_t.T,
        pg[:4], pg[4], bg[:4], bg[4], dg[0], dg[1], skip_grad, gategain_grad, outproj_grad)


def solution(mesh):
    batch, tensor = mesh.shape["batch"], mesh.shape["tensor"]
    z = batch // 4
    split = Mesh(mesh.devices.reshape(z, 2, 2, tensor), ("z", "x", "core", "tensor"))
    rows = ("z", "x", "core")
    placed = (
        P(rows, "tensor", None), P(rows, None), P(), P(None, "tensor"), P(None, "tensor"), P(),
        P(None, "tensor"), P(None, "tensor"), P("tensor"), P(), P(), P("tensor"), P("tensor"),
        P("tensor"), P("tensor"), P("tensor", None), P(rows, "tensor", None))
    given = (
        P(rows, "tensor", None), P(rows, "tensor", None), P(), P(None, "tensor"), P(None, "tensor"),
        P(), P(None, "tensor"), P(None, "tensor"), P("tensor"), P(), P(), P("tensor"), P("tensor"),
        P("tensor"), P("tensor"), P("tensor", None))
    return jax.shard_map(
        functools.partial(shards, tensor), mesh=split, in_specs=placed, out_specs=given,
        check_vma=False)
```

time: 1840 us -> 1050 us (0.57)
  waiting for transfers between devices: 891 us -> 590 us
  local copies, waits for them, and re-layouts: 240 us -> 12.9 us
  matrix products: 358 us -> 144 us
  Pallas kernels: 0 us -> 102 us
  other arithmetic: 174 us -> 77.9 us
  blocking collectives: 159 us -> 105 us
    psum x1 -> x3, waiting for transfers between devices: 839 us -> 457 us  [the longest x1 399 us: shards(): zproj_grad = lax.psum(zproj_part, every).astype(F32)]
    dot_general x27 -> x11, matrix products: 358 us -> 144 us  [the longest x4 49.7 us: dot_nt(): lax.dot_general(a, b, (((1,), (1,)), ((), ())), preferred_element_type=F32)]
    reshape x16 -> x0, local copies, waits for them, and re-layouts: 149 us -> none  [the longest x4 57.6 us: mixer(): heads_view = xconv.reshape(row_count, length, head_count, head_size)]
    pallas_call x0 -> x4, Pallas kernels: none -> 102 us  [the longest x1 54.9 us: bwd(): pl.pallas_call(functools.partial(bwd_kernel, heads, head_size, state, fir...]
    reduce_sum x12 -> x3, other arithmetic: 66.6 us -> 5.67 us  [the longest x1 4.3 us: shards(): normgain_part = jnp.sum(grad_normed * residual * inv_rms, axis=(0, 1))]
    psum x5 -> x3, blocking collectives: 159 us -> 105 us  [the longest x1 58.8 us: shards(): lax.psum((small_part[2 * state:2 * state + heads], pg[:5], dg[:2, :heads]...]
    reduce_scatter x1, waiting for transfers between devices: 0.01 us -> 52.1 us  [shards(): lax.psum_scatter(partial_out, 'tensor', scatter_dimension=1, tiled=True)]
    unnamed x243 -> x63, local copies, waits for them, and re-layouts: 44.5 us -> 5.93 us
  transfers between devices with their start and end apart: 5 -> 7, of which waited for: 2 -> 5; matrix products, arithmetic and copies ran while one was open for 19% -> 18% of each run, Pallas kernels for 0% -> 4%
where the time goes in v1:
time: 1050 us
  waiting for transfers between devices  590 us (56%)
  matrix products  144 us (14%)
  blocking collectives  105 us (10%)
  Pallas kernels  102 us (10%)
  other arithmetic  77.9 us (7%)
  between operations  14.9 us (1%)
  local copies, waits for them, and re-layouts  12.9 us (1%)
    psum x1, waiting for transfers between devices, shards(): zproj_grad = lax.psum(zproj_part, every).astype(F32)  399 us
    psum x1, blocking collectives, shards(): lax.psum((small_part[2 * state:2 * state + heads], pg[:5], dg[:2, :heads]...  58.8 us
    psum x1, waiting for transfers between devices, shards(): lax.psum((small_part[2 * state:2 * state + heads], pg[:5], dg[:2, :heads]...  58.3 us
    pallas_call x1, Pallas kernels, bwd(): pl.pallas_call(functools.partial(bwd_kernel, heads, head_size, state, fir...  54.9 us
    reduce_scatter x1, waiting for transfers between devices, shards(): lax.psum_scatter(partial_out, 'tensor', scatter_dimension=1, tiled=True)  52.1 us
    dot_general x4, matrix products, dot_nt(): lax.dot_general(a, b, (((1,), (1,)), ((), ())), preferred_element_type=F32)  49.7 us
    dot_general x4, matrix products, dot_tn(): lax.dot_general(a, b, (((0,), (0,)), ((), ())), preferred_element_type=F32)  49.3 us
    all_gather x1, waiting for transfers between devices, shards(): gathered = lax.all_gather(normed_low, 'tensor', axis=1, tiled=True)  48.7 us
  transfers between devices with their start and end apart: 7, of which 5 were waited for; matrix products, arithmetic and copies ran while one was open for 18% of the time, Pallas kernels for 4%

profile of v1, /device:TPU:1, one launch (start us, length us, event | category | flops | bytes accessed | tf_op | source)
XLA Modules:
  0.0 1046.3 jit_solution(13110982660198695739)
XLA Ops:
  23.2 48.7 %all-gather.3.cloned.1.call-done = bf16[1,1024,2048]{2,1,0:T(8,128)(2,1)} async-done(((bf16[1,512,2048]{2,1,0:T(8,128)(2,1)}), bf16[1,1024,2048]{2,1,0:T(8,128)(2,1)}) %all-gather.3.cloned.1.call-update) | async-done | bytes 4194320 | tf_op jit(solution)/shard_map/all_gather | solution.py:514
  71.9 14.5 %fusion.27.z = f32[1024,2048]{1,0:T(8,128)} fusion(bf16[2048,2048]{1,0:T(8,128)(2,1)} %param.20, bf16[1,1024,2048]{2,1,0:T(8,128)(2,1)} %all-gather.3.cloned.1.call-done), kind=kOutput, calls=%fused_computation.75 | convolution fusion | flops 8589934592 | bytes 20971520 | tf_op jit(solution)/shard_map/dot_general | solution.py:19
  86.3 11.1 %prep.1 = (f32[1024,384]{1,0:T(8,128)}, bf16[1024,256]{1,0:T(8,128)(2,1)}, bf16[128,1024]{1,0:T(8,128)(2,1)}, bf16[128,1024]{1,0:T(8,128)(2,1)}, f32[1024,128]{1...) custom-call(bf16[1024,2048]{1,0:T(8,128)(2,1)} %bitcast.73, bf16[2048,384]{1,0:T(8,128)(2,1)} %fusion.13.wcat, ...), custom_call_target="tpu_custom_call" | custom-call | flops 1610612736 | bytes 8388608 | tf_op jit(solution)/shard_map/prep/pallas_call | solution.py:108
  97.4 13.2 %fusion.29.x = f32[1024,2048]{1,0:T(8,128)} fusion(bf16[2048,2048]{1,0:T(8,128)(2,1)} %param.21, bf16[1,1024,2048]{2,1,0:T(8,128)(2,1)S(1)} %copy-done.1), kind=kOutput, calls=%fused_computation.77 | convolution fusion | flops 8589934592 | bytes 20971520 | tf_op jit(solution)/shard_map/dot_general | solution.py:19
  111.2 29.0 %scan_forward.1 = (f32[1024,2048]{1,0:T(8,128)}, bf16[8,128,2048]{2,1,0:T(8,128)(2,1)}, f32[1024,128]{1,0:T(8,128)}) custom-call(f32[1024,2048]{1,0:T(8,128)} %fusion.29.x, f32[1024,2048]{1,0:T(8,128)} %fusion.27.z, f32[1024,128]{1,0:T(8,128)} %select_select_fusion.meta, f32[8,1024]{1,0:T(8,128)} %broadcast_in_dim.81.segrow, ...), custom_call_target="tpu_custom_call" | custom-call | flops 21474836480 | bytes 33554432 | tf_op jit(solution)/shard_map/scan_forward/pallas_call | solution.py:232
  141.6 19.2 %multiply_reduce_fusion.1 = (f32[1024]{0:T(1024)S(1)}, f32[1024,2048]{1,0:T(8,128)}) fusion(f32[2048]{0:T(1024)S(1)} %copy-done.18, f32[1024,2048]{1,0:T(8,128)} %get-tuple-element.39.scan, f32[1024,2048]{1,0:T(8,128)} %fusion.27.z, bf16[2048,2048]{1,0:T(8,128)(2,1)} %param.32, bf16[1,1024,2048]{2,1,0:T(8,128)(2,1)} %all-gather.5.cloned.1.call-done), kind=kOutput, calls=%fused_computation.6 | convolution fusion | flops 8606710784 | bytes 37761024 | tf_op jit(solution)/shard_map/dot_general | solution.py:23
  164.6 16.3 %multiply_convert_fusion.1 = (bf16[1024,2048]{1,0:T(8,128)(2,1)}, bf16[1024,2048]{1,0:T(8,128)(2,1)}, f32[2048]{0:T(1024)}) fusion(f32[1024,2048]{1,0:T(8,128)} %fusion.27.z, f32[1024,2048]{1,0:T(8,128)} %get-tuple-element.39.scan, f32[1024]{0:T(1024)S(1)} %fusion.15, f32[1024,2048]{1,0:T(8,128)} %get-tuple-element.96, f32[1024]{0:T(1024)S(1)} %bitcast.83, ...), kind=kLoop, calls=%fused_computation.3 | loop fusion | flops 44038144 | bytes 33579008 | tf_op jit(solution)/shard_map/convert_element_type | solution.py:546
  181.0 54.9 %scan_backward.1 = (bf16[1024,2048]{1,0:T(8,128)(2,1)}, f32[1024,256]{1,0:T(8,128)}, f32[1024,128]{1,0:T(8,128)}, f32[1024,128]{1,0:T(8,128)}, f32[8,2048]{1,0:T(8,128)}) custom-call(f32[1024,2048]{1,0:T(8,128)} %fusion.29.x, bf16[1024,2048]{1,0:T(8,128)(2,1)} %get-tuple-element.80.dy, f32[1024,2048]{1,0:T(8,128)} %get-tuple-element.39.scan, ...), custom_call_target="tpu_custom_call" | custom-call | flops 42949672960 | bytes 33554432 | tf_op jit(solution)/shard_map/scan_backward/pallas_call | solution.py:370
  247.0 13.2 %fusion.34 = f32[1024,2048]{1,0:T(8,128)S(1)} fusion(bf16[1024,2048]{1,0:T(8,128)(2,1)} %get-tuple-element.79, bf16[2048,2048]{1,0:T(8,128)(2,1)} %param.20), kind=kOutput, calls=%fused_computation.79 | convolution fusion | flops 8589934592 | bytes 20971520 | tf_op jit(solution)/shard_map/dot_general | solution.py:23
  260.2 11.4 %fusion.35 = f32[1024,2048]{1,0:T(8,128)S(1)} fusion(bf16[1024,2048]{1,0:T(8,128)(2,1)S(1)} %copy-done.28, bf16[2048,2048]{1,0:T(8,128)(2,1)} %param.21), kind=kOutput, calls=%fused_computation.80 | convolution fusion | flops 8589934592 | bytes 20971520 | tf_op jit(solution)/shard_map/dot_general | solution.py:23
  277.6 17.2 %convert_bitcast_fusion = bf16[1,1024,2048]{2,1,0:T(8,128)(2,1)} fusion(bf16[2048,2048]{1,0:T(8,128)(2,1)} %param.32, f32[1024]{0:T(1024)S(1)} %bitcast.84, f32[2048]{0:T(1024)S(1)} %copy-done.18, f32[1024,2048]{1,0:T(8,128)} %get-tuple-element.39.scan, f32[1024,2048]{1,0:T(8,128)} %fusion.27.z), kind=kOutput, calls=%fused_computation.25 | convolution fusion | flops 8608808960 | bytes 29372416 | tf_op jit(solution)/shard_map/dot_general | solution.py:19
  294.9 14.5 %convolution_convert_fusion.1 = bf16[2048,2048]{1,0:T(8,128)(2,1)} fusion(bf16[1024,2048]{1,0:T(8,128)(2,1)} %get-tuple-element.43, bf16[1,1024,2048]{2,1,0:T(8,128)(2,1)} %all-gather.3.cloned.1.call-done), kind=kOutput, calls=%fused_computation.10 | convolution fusion | flops 8594128896 | bytes 16777216 | tf_op jit(solution)/shard_map/dot_general | solution.py:27
  309.4 11.4 %convolution_convert_fusion.2 = bf16[2048,2048]{1,0:T(8,128)(2,1)} fusion(bf16[1024,2048]{1,0:T(8,128)(2,1)S(1)} %copy-done.7, bf16[1,1024,2048]{2,1,0:T(8,128)(2,1)S(1)} %copy-done.3), kind=kOutput, calls=%fused_computation.11 | convolution fusion | flops 8594128896 | bytes 16777216 | tf_op jit(solution)/shard_map/dot_general | solution.py:27
  320.9 20.5 %convolution_convert_fusion = bf16[2048,2048]{1,0:T(8,128)(2,1)} fusion(bf16[1,1024,2048]{2,1,0:T(8,128)(2,1)S(1)} %copy-done.27, f32[1024]{0:T(1024)S(1)} %bitcast.85, f32[2048]{0:T(1024)S(1)} %copy-done.18, f32[1024,2048]{1,0:T(8,128)} %get-tuple-element.39.scan, f32[1024,2048]{1,0:T(8,128)} %fusion.27.z), kind=kOutput, calls=%fused_computation.9 | convolution fusion | flops 8610906112 | bytes 29372416 | tf_op jit(solution)/shard_map/dot_general | solution.py:27
  342.4 58.8 %all-reduce.5 = (f32[5,2048]{1,0:T(8,128)S(1)}, f32[2,32]{1,0:T(2,128)S(1)}, f32[32]{0:T(128)}, f32[2048]{0:T(1024)}) all-reduce(f32[5,2048]{1,0:T(8,128)S(1)} %bitcast.81, f32[2,32]{1,0:T(2,128)S(1)} %slice.78, f32[32]{0:T(128)S(1)} %reduce_sum.68, ...), channel_id=1, replica_groups=mesh['z'=4,'x'=2,'core'=2,'tensor'=2] {'z','x','core'}, use_global_device_ids=true, to_apply=%region_13.14 | all-reduce | flops 12384 | bytes 99072 | tf_op jit(solution)/shard_map/psum | solution.py:579
  406.8 31.7 %reduce-scatter.5.cloned.1.call-done = bf16[1,512,2048]{2,1,0:T(8,128)(2,1)} async-done(((bf16[1,1024,2048]{2,1,0:T(8,128)(2,1)}), bf16[1,512,2048]{2,1,0:T(8,128)(2,1)}) %reduce-scatter.5.cloned.1.call-update) | async-done | bytes 2097168 | tf_op jit(solution)/shard_map/reduce_scatter | solution.py:567
  442.8 52.1 %reduce-scatter.3.cloned.1.call-done = bf16[1,512,2048]{2,1,0:T(8,128)(2,1)} async-done(((bf16[1,1024,2048]{2,1,0:T(8,128)(2,1)}), bf16[1,512,2048]{2,1,0:T(8,128)(2,1)}) %reduce-scatter.3.cloned.1.call-update) | async-done | bytes 2097168 | tf_op jit(solution)/shard_map/reduce_scatter | solution.py:555
  495.0 6.7 fusion.4
  501.7 42.0 %all-reduce.4 = (f32[2048]{0:T(1024)}, f32[8,256]{1,0:T(8,128)S(1)}) all-reduce(f32[2048]{0:T(1024)S(1)} %get-tuple-element.68, f32[8,256]{1,0:T(8,128)S(1)} %copy-done.21), channel_id=1, replica_groups=mesh['z'=4,'x'=2,'core'=2,'tensor'=2] {'z','x','core','tensor'}, use_global_device_ids=true, to_apply=%region_8.9 | all-reduce | flops 4096 | bytes 32768 | tf_op jit(solution)/shard_map/psum | solution.py:577
  544.8 399.2 %all-reduce.15.cloned.1.call-done = (bf16[2048,2048]{1,0:T(8,128)(2,1)}, bf16[2048,2048]{1,0:T(8,128)(2,1)}, bf16[2048,2048]{1,0:T(8,128)(2,1)}) async-done(((bf16[2048,2048]{1,0:T(8,128)(2,1)}, bf16[2048,2048]{1,0:T(8,128)(2,1)}, bf16[2048,2048]{1,0:T(8,128)(2,1)}), (bf16[2048,2048]{1,0:T(8,128)(2,1)}, bf16[2048,2048]{1,0:T(8,128)(2,1)}, bf16[2048,2048]{1,0:T(8,128)(2,1)})) %all-reduce.15.cloned.1.call-update) | async-done | bytes 25165840 | tf_op jit(solution)/shard_map/psum | solution.py:552
  944.0 11.7 %convert_element_type.104 = f32[2048,2048]{1,0:T(8,128)} convert(bf16[2048,2048]{1,0:T(8,128)(2,1)} %get-tuple-element.76) | non-fusion elementwise | flops 4194304 | bytes 25165824 | tf_op jit(solution)/shard_map/convert_element_type | solution.py:552
  955.7 11.7 %convert_element_type.106 = f32[2048,2048]{1,0:T(8,128)} convert(bf16[2048,2048]{1,0:T(8,128)(2,1)} %get-tuple-element.77) | non-fusion elementwise | flops 4194304 | bytes 25165824 | tf_op jit(solution)/shard_map/convert_element_type | solution.py:562
  967.4 11.7 %convert_element_type.108 = f32[2048,2048]{1,0:T(8,128)} convert(bf16[2048,2048]{1,0:T(8,128)(2,1)} %get-tuple-element.78) | non-fusion elementwise | flops 4194304 | bytes 25165824 | tf_op jit(solution)/shard_map/convert_element_type | solution.py:550
  979.1 58.3 %all-reduce.13.cloned.1.call-done = f32[2048,32]{0,1:T(8,128)} async-done(((f32[2048,32]{0,1:T(8,128)}), f32[2048,32]{0,1:T(8,128)}) %all-reduce.13.cloned.1.call-update) | async-done | bytes 262160 | tf_op jit(solution)/shard_map/psum | solution.py:579
  (125 shorter events, 52.5 us)
Async XLA Ops:
  7.2 64.7 %all-gather.3.cloned.1.call-start = ((), (), s32[]{:S(2)}) async-start(), calls=%async_computation.2 | async-start | bytes 6291456 | tf_op jit(solution)/shard_map/all_gather | solution.py:514
  12.9 5.1 copy-start.25
  12.9 5.1 copy-start.26
  12.9 5.8 copy-start.8
  12.9 128.6 %all-gather.5.cloned.1.call-start = ((), (), s32[]{:S(2)}) async-start(), calls=%async_computation.3 | async-start | bytes 6291456 | tf_op jit(solution)/shard_map/all_gather | solution.py:519
  17.0 386.8 %all-reduce.11.cloned.1.call-start = ((), (), s32[]{:S(2)}) async-start(), calls=%async_computation.6 | async-start | bytes 4194304 | tf_op jit(solution)/shard_map/psum | solution.py:577
  18.0 68.3 %copy-start.5 = (bf16[2048,32]{1,0:T(8,128)(2,1)}, bf16[2048,32]{1,0:T(8,128)(2,1)S(1)}, u32[]{:S(2)}) copy-start(bf16[2048,32]{1,0:T(8,128)(2,1)S(1)} %copy.35) | copy-start | bytes 393220
  86.3 11.1 %copy-start.1 = (bf16[1,1024,2048]{2,1,0:T(8,128)(2,1)S(1)}, bf16[1,1024,2048]{2,1,0:T(8,128)(2,1)}, u32[]{:S(2)}) copy-start(bf16[1,1024,2048]{2,1,0:T(8,128)(2,1)} %all-gather.3.cloned.1.call-done) | copy-start | bytes 12582916
  111.2 30.3 %copy-start.18 = (f32[2048]{0:T(1024)S(1)}, f32[2048]{0:T(1024)}, u32[]{:S(2)}) copy-start(f32[2048]{0:T(1024)} %param.31) | copy-start | bytes 24580
  235.9 6.6 copy-start.2
  246.9 191.6 %reduce-scatter.5.cloned.1.call-start = ((), (), s32[]{:S(2)}) async-start(), calls=%async_computation.5 | async-start | bytes 6291456 | tf_op jit(solution)/shard_map/reduce_scatter | solution.py:567
  247.0 13.2 %copy-start.28 = (bf16[1024,2048]{1,0:T(8,128)(2,1)S(1)}, bf16[1024,2048]{1,0:T(8,128)(2,1)}, u32[]{:S(2)}) copy-start(bf16[1024,2048]{1,0:T(8,128)(2,1)} %get-tuple-element.43) | copy-start | bytes 12582916
  260.2 11.4 %copy-start.6 = (bf16[2048,32]{1,0:T(8,128)(2,1)S(1)}, bf16[2048,32]{1,0:T(8,128)(2,1)}, u32[]{:S(2)}) copy-start(bf16[2048,32]{1,0:T(8,128)(2,1)} %copy-done.5) | copy-start | bytes 393220
  277.6 217.4 %reduce-scatter.3.cloned.1.call-start = ((), (), s32[]{:S(2)}) async-start(), calls=%async_computation.4 | async-start | bytes 6291456 | tf_op jit(solution)/shard_map/reduce_scatter | solution.py:555
  294.9 649.2 %all-reduce.15.cloned.1.call-start = ((), (), s32[]{:S(2)}) async-start(), calls=%async_computation.8 | async-start | bytes 50331648 | tf_op jit(solution)/shard_map/psum | solution.py:552
  294.9 14.5 %copy-start.3 = (bf16[1,1024,2048]{2,1,0:T(8,128)(2,1)S(1)}, bf16[1,1024,2048]{2,1,0:T(8,128)(2,1)}, u32[]{:S(2)}) copy-start(bf16[1,1024,2048]{2,1,0:T(8,128)(2,1)} %all-gather.3.cloned.1.call-done) | copy-start | bytes 12582916
  294.9 14.5 %copy-start.7 = (bf16[1024,2048]{1,0:T(8,128)(2,1)S(1)}, bf16[1024,2048]{1,0:T(8,128)(2,1)}, u32[]{:S(2)}) copy-start(bf16[1024,2048]{1,0:T(8,128)(2,1)} %get-tuple-element.79) | copy-start | bytes 12582916
  309.4 11.4 %copy-start.27 = (bf16[1,1024,2048]{2,1,0:T(8,128)(2,1)S(1)}, bf16[1,1024,2048]{2,1,0:T(8,128)(2,1)}, u32[]{:S(2)}) copy-start(bf16[1,1024,2048]{2,1,0:T(8,128)(2,1)} %all-gather.5.cloned.1.call-done) | copy-start | bytes 12582916
  341.4 97.1 %copy-start.13 = (f32[2048]{0:T(1024)S(1)}, f32[2048]{0:T(1024)}, u32[]{:S(2)}) copy-start(f32[2048]{0:T(1024)} %param.19) | copy-start | bytes 24580
  341.4 97.1 %copy-start.15 = (f32[512]{0:T(512)S(1)}, f32[512]{0:T(512)}, u32[]{:S(2)}) copy-start(f32[512]{0:T(512)} %copy-done.14) | copy-start | bytes 6148
  341.4 696.0 %all-reduce.13.cloned.1.call-start = ((), (), s32[]{:S(2)}) async-start(), calls=%async_computation.7 | async-start | bytes 524288 | tf_op jit(solution)/shard_map/psum | solution.py:579
  406.8 88.1 %copy-start.19 = (f32[512]{0:T(512)S(1)}, f32[512]{0:T(512)}, u32[]{:S(2)}) copy-start(f32[512]{0:T(512)} %get-tuple-element.91) | copy-start | bytes 6148
  438.5 56.5 %copy-start.4 = (bf16[1,512,2048]{2,1,0:T(8,128)(2,1)S(1)}, bf16[1,512,2048]{2,1,0:T(8,128)(2,1)}, u32[]{:S(2)}) copy-start(bf16[1,512,2048]{2,1,0:T(8,128)(2,1)} %reduce-scatter.5.cloned.1.call-done) | copy-start | bytes 6291460
  495.0 6.7 copy-start.21
  (12 other events, 37.9 us)
Sparse Core Ops, SparseCore 0:
  13.0 58.8 all-gather.2
  74.0 56.7 all-gather.4
  247.0 134.0 all-reduce.10
  384.0 54.4 reduce-scatter.4
  440.6 54.2 reduce-scatter.2
  500.9 443.0 all-reduce.14
  948.4 88.9 all-reduce.12
